TPU v7x, 32 devices: a whole 2x2x4 slice. The times are simulated.
32 devices in a mesh: gx: 4 (over z), gy: 4 (over x, core), gz: 2 (over y).
Axes of the slice: x: 2, y: 2, z: 4, core: 2. Of those that a mesh axis runs over, the one named last changes fastest.
Arguments:
- populations: float32 [19, 16, 128, 512], P(None, 'gz', 'gy', 'gx'), as said below
- rbf_weights: bfloat16 [2048, 128, 128], P(('gx', 'gy', 'gz')), may hold values from -0.5 to 0.5
- owner_map: int32 [2048, 1], P(('gx', 'gy', 'gz')), may hold values from 0 to 7; in each aligned block of 64 rows (0 to 63, 64 to 127, ...) at most 16 rows name the same one
- shell_slot: int32 [2048, 1], P(('gx', 'gy', 'gz')), may hold values from 0 to 7
- compliance: float32 [256, 128, 128], P(('gx', 'gy', 'gz')), may hold values from -0.5 to 0.5
- neighbour_compliance: float32 [4096, 128], P(('gx', 'gy', 'gz')), may hold values from -0.5 to 0.5
- interface_row: int32 [2048], P(('gx', 'gy', 'gz')), may hold values from 0 to 255, as said below
Outputs:
- new_populations: float32 [19, 16, 128, 512], P(None, 'gz', 'gy', 'gx')
- displacement: float32 [256, 3, 128], P(('gx', 'gy', 'gz'))
- wall_motion: float32 [2048, 3, 128], P(('gx', 'gy', 'gz'))
Inputs may be any that keep to these rules, and one draw needn't show every extreme that they name: `populations`: each population lies between 0.5 and 1.5 times its lattice weight. `owner_map`: among the 64 rows of one device no owner appears more than 16 times, and some owner appears exactly 16 times. `interface_row`: the 64 rows of one device are distinct.
All inputs are finite; a program needn't handle non-finite values.
Results may differ from a plain program's by a relative error of at most 0.004.
Values sent between devices are 32-bit elements; how exact they have to be, the bound alone decides.
A program may use at most 64 MiB of HBM per device.

v0:
```python
import jax
import jax.numpy as jnp
from jax import lax
from jax.sharding import PartitionSpec as P

lattice_velocity = (
    (0, 0, 0),
    (1, 0, 0),
    (-1, 0, 0),
    (0, 1, 0),
    (0, -1, 0),
    (0, 0, 1),
    (0, 0, -1),
    (1, 1, 0),
    (-1, -1, 0),
    (1, -1, 0),
    (-1, 1, 0),
    (1, 0, 1),
    (-1, 0, -1),
    (1, 0, -1),
    (-1, 0, 1),
    (0, 1, 1),
    (0, -1, -1),
    (0, 1, -1),
    (0, -1, 1),
)
lattice_weight = (1.0 / 3.0,) + (1.0 / 18.0,) * 6 + (1.0 / 36.0,) * 12
load_scale = 30.0
relaxation = 1.6


def padded_2(block, sides, width):
    for axis, dim in sides:
        count = lax.axis_size(axis)
        forward = [(i, i + 1) for i in range(count - 1)]
        forward.append((count - 1, 0))
        backward = [(target, source) for source, target in forward]
        low = lax.ppermute(
            lax.slice_in_dim(block, block.shape[dim] - width, None, axis=dim), axis, forward
        )
        high = lax.ppermute(lax.slice_in_dim(block, 0, width, axis=dim), axis, backward)
        block = jnp.concatenate([low, block, high], axis=dim)
    return block


def from_behind(array, axis, by):
    peers = lax.axis_size(axis)
    pairs = [(i, i + by) for i in range(peers) if 0 <= i + by < peers]
    return lax.ppermute(array, axis, pairs)


def moment_matrix():
    return jnp.array(
        [
            [1.0] * 19,
            [float(item[0]) for item in lattice_velocity],
            [float(item[1]) for item in lattice_velocity],
            [float(item[2]) for item in lattice_velocity],
        ],
        dtype=jnp.float32,
    )


def collide(flattened):
    moments = jnp.dot(moment_matrix(), flattened, precision=lax.Precision.HIGHEST)
    density = moments[0]
    velocity = moments[1:4] / density
    speed_square = velocity[0] * velocity[0] + velocity[1] * velocity[1] + velocity[2] * velocity[2]
    relaxed = []
    for direction in range(19):
        along_x, along_y, along_z = lattice_velocity[direction]
        projected = along_x * velocity[0] + along_y * velocity[1] + along_z * velocity[2]
        equilibrium = (
            lattice_weight[direction]
            * density
            * (1.0 + 3.0 * projected + 4.5 * projected * projected - 1.5 * speed_square)
        )
        relaxed.append(flattened[direction] - relaxation * (flattened[direction] - equilibrium))
    return (relaxed, moments)


def moving_set(component):
    return [direction for direction in range(19) if lattice_velocity[direction][component] != 0]


def place_moved(current, padded, component, array_dim):
    length = current[0].shape[array_dim - 1]
    updated = list(current)
    for position, direction in enumerate(moving_set(component)):
        offset = 1 - lattice_velocity[direction][component]
        updated[direction] = lax.slice_in_dim(
            padded[position], offset, offset + length, axis=array_dim - 1
        )
    return updated


def body(
    populations, rbf_weights, owner_map, shell_slot, compliance, neighbour_compliance, interface_row
):
    local_shape = populations.shape[1:]
    depth, height, width = local_shape
    relaxed, moments = collide(populations.reshape(19, -1))
    relaxed = [item.reshape(local_shape) for item in relaxed]
    current = relaxed
    part_x = jnp.stack([current[direction] for direction in moving_set(0)])
    padded_x = padded_2(part_x, (("gx", 3),), 1)
    current = place_moved(current, padded_x, 0, 3)
    part_y = jnp.stack([current[direction] for direction in moving_set(1)])
    padded_y = padded_2(part_y, (("gy", 2),), 1)
    current = place_moved(current, padded_y, 1, 2)
    part_z = jnp.stack([current[direction] for direction in moving_set(2)])
    padded_z = padded_2(part_z, (("gz", 1),), 1)
    current = place_moved(current, padded_z, 2, 1)
    new_populations = jnp.stack(current)
    block_count = rbf_weights.shape[0]
    node_count = rbf_weights.shape[2]
    shell_count = compliance.shape[0]
    pencils = lax.axis_size("gy")
    blocks_z = lax.axis_size("gz")
    owner_count = pencils * blocks_z
    capacity = max(2, 2 * block_count // owner_count)
    slots = owner_count * capacity
    momentum = moments[1:4].reshape(3, depth * height, width)
    interface_momentum = jnp.take(momentum, interface_row, axis=1)
    traction = (load_scale * interface_momentum).astype(jnp.bfloat16)
    forces = jnp.einsum("kbc,bcs->bks", traction, rbf_weights, preferred_element_type=jnp.float32)
    forces = forces.reshape(block_count, 3 * node_count)
    owner_of = owner_map[:, 0]
    owner_onehot = (owner_of[:, None] == jnp.arange(owner_count, dtype=jnp.int32)[None, :]).astype(
        jnp.float32
    )
    running = jnp.cumsum(owner_onehot, axis=0) - owner_onehot
    slot_rank = jnp.sum(running * owner_onehot, axis=1).astype(jnp.int32)
    slot_index = owner_of * capacity + slot_rank
    placement = (jnp.arange(slots, dtype=jnp.int32)[:, None] == slot_index[None, :]).astype(
        jnp.float32
    )
    outgoing = jnp.dot(placement, forces, precision=lax.Precision.HIGHEST)
    outgoing_tags = (
        jnp.dot(
            placement, (shell_slot[:, 0] + 1).astype(jnp.float32), precision=lax.Precision.HIGHEST
        )
        - 1.0
    )
    incoming, slot_tags = (
        lax.all_to_all(
            outgoing.reshape(owner_count, capacity, 3 * node_count),
            ("gy", "gz"),
            split_axis=0,
            concat_axis=0,
            tiled=True,
        ),
        lax.all_to_all(
            outgoing_tags.reshape(owner_count, capacity),
            ("gy", "gz"),
            split_axis=0,
            concat_axis=0,
            tiled=True,
        ),
    )
    incoming = incoming.reshape(slots, 3 * node_count)
    slot_tags = slot_tags.reshape(slots)
    selector = (slot_tags[None, :] == jnp.arange(shell_count, dtype=jnp.float32)[:, None]).astype(
        jnp.float32
    )
    loads = jnp.dot(selector, incoming, precision=lax.Precision.HIGHEST).reshape(
        shell_count, 3, node_count
    )
    previous = from_behind(loads[shell_count - 1], ("gy", "gz"), 1)
    displacement = jnp.einsum("skn,snm->skm", loads, compliance, precision=lax.Precision.HIGHEST)
    shared_term = jnp.dot(previous, neighbour_compliance, precision=lax.Precision.HIGHEST)
    displacement = displacement.at[0].add(shared_term)
    returned = jnp.dot(
        selector.T,
        displacement.reshape(shell_count, 3 * node_count),
        precision=lax.Precision.HIGHEST,
    )
    arrived = lax.all_to_all(
        returned.reshape(owner_count, capacity, 3 * node_count),
        ("gy", "gz"),
        split_axis=0,
        concat_axis=0,
        tiled=True,
    )
    own_motion = jnp.dot(
        placement.T, arrived.reshape(slots, 3 * node_count), precision=lax.Precision.HIGHEST
    )
    own_motion = own_motion.reshape(block_count, 3, node_count).astype(jnp.bfloat16)
    wall_motion = jnp.einsum(
        "bks,bcs->bkc", own_motion, rbf_weights, preferred_element_type=jnp.float32
    )
    return (new_populations, displacement, wall_motion)


def solution(mesh):
    return jax.shard_map(
        body,
        mesh=mesh,
        in_specs=(
            P(None, "gz", "gy", "gx"),
            P(("gx", "gy", "gz"), None, None),
            P(("gx", "gy", "gz"), None),
            P(("gx", "gy", "gz"), None),
            P(("gx", "gy", "gz"), None, None),
            P(("gx", "gy", "gz"), None),
            P(("gx", "gy", "gz")),
        ),
        out_specs=(
            P(None, "gz", "gy", "gx"),
            P(("gx", "gy", "gz"), None, None),
            P(("gx", "gy", "gz"), None, None),
        ),
        check_vma=False,
    )
```

profile of v0, /device:TPU:1, one launch (start us, length us, event | category | flops | bytes accessed | tf_op | source)
XLA Modules:
  0.0 100.6 jit_solution(7455229284284190461)
XLA Ops:
  4.7 5.2 %all-to-all-start = ((f32[8,1,16]{2,1,0:T(1,128)}), f32[8,1,16]{2,1,0:T(1,128)S(1)}, u32[]{:S(2)}, u32[]{:S(2)}) async-start(f32[8,1,16]{2,1,0:T(1,128)} %bitcast.50), calls=%async_computation | async-start | bytes 8192 | tf_op jit(solution)/shard_map/all_to_all | solution.py:153
  9.9 2.0 %pad.24 = f32[24,256,128]{2,1,0:T(8,128)S(1)} pad(f32[19,256,128]{2,1,0:T(8,128)} %bitcast.214, f32[]{:T(128)} %constant.62.clone.1), padding=0_5x0_0x0_0 | pad | bytes 5636100
  11.9 1.8 %copy.114 = f32[3,8,256,128]{3,1,2,0:T(8,128)S(1)} copy(f32[3,8,256,128]{3,2,1,0:T(8,128)S(1)} %bitcast.213) | data formatting | bytes 6291456
  13.8 1.8 %fusion.181 = f32[4,32768]{1,0:T(4,128)S(1)} fusion(f32[4,19]{1,0:T(4,128)S(1)} %copy-done.16, f32[19,32768]{1,0:T(8,128)S(1)} %bitcast.212), kind=kOutput, calls=%fused_computation.286 | convolution fusion | flops 29884416 | bytes 3014960 | tf_op jit(solution)/shard_map/dot_general | solution.py:65
  20.4 2.0 %fusion.179 = (f32[10,8,32,1]{3,2,1,0:T(8,128)}, f32[10,8,32,1]{3,2,1,0:T(8,128)}) fusion(f32[10,8,32,128]{3,2,1,0:T(8,128)S(1)} %fusion.80), kind=kLoop, calls=%fused_computation.284 | loop fusion | bytes 40960 | tf_op jit(solution)/shard_map/slice | solution.py:39
  22.3 2.5 %copy.113 = f32[10,8,32,1]{2,1,3,0:T(8,128)} copy(f32[10,8,32,1]{3,2,1,0:T(8,128)} %get-tuple-element.60) | data formatting | bytes 20480
  24.8 3.3 %collective-permute-start.1 = (f32[10,8,32,1]{2,1,3,0:T(8,128)}, f32[10,8,32,1]{2,1,3,0:T(8,128)}, u32[]{:S(2)}, u32[]{:S(2)}) collective-permute-start(f32[10,8,32,1]{2,1,3,0:T(8,128)} %copy.113), channel_id=1, source_target_pairs={{8,0},{16,8},{24,16},{0,24},{9,1},{17,9},{25,17},{1,25},{10,2},{18... | collective-permute-start | bytes 30728 | tf_op jit(solution)/shard_map/ppermute | solution.py:41
  28.1 2.5 %copy.112 = f32[10,8,32,1]{2,1,3,0:T(8,128)} copy(f32[10,8,32,1]{3,2,1,0:T(8,128)} %get-tuple-element.59) | data formatting | bytes 20480
  31.1 2.3 %gather_fusion = f32[64,3,128]{2,1,0:T(4,128)} fusion(f32[3,256,128]{2,0,1:T(4,128)} %get-tuple-element.61, s32[1024]{0:T(1024)S(1)} %pad_clamp_fusion), kind=kCustom, calls=%fused_computation | custom fusion | bytes 196864 | tf_op jit(solution)/shard_map/jit(_take)/gather | solution.py:124
  33.4 2.3 %fusion.149 = f32[64,3,128]{2,1,0:T(4,128)} fusion(bf16[64,128,128]{2,1,0:T(8,128)(2,1)S(1)} %copy-done, f32[64,3,128]{2,1,0:T(4,128)} %gather_fusion, pred[64]{0:T(512)(128)(4,1)} %compare_and_fusion), kind=kOutput, calls=%fused_computation.242 | convolution fusion | flops 6365184 | bytes 2293824 | tf_op jit(solution)/shard_map/kbc,bcs->bks/dot_general | solution.py:126
  35.7 1.6 %reshape.1280 = f32[64,384,1]{1,0,2:T(8,128)} reshape(f32[64,3,128]{2,1,0:T(4,128)} %fusion.149) | data formatting | bytes 196608 | tf_op jit(solution)/shard_map/reshape | solution.py:127
  37.3 1.9 %fusion.156 = f32[8,16,384]{2,1,0:T(8,128)} fusion(f32[64,384,1]{1,0,2:T(8,128)} %reshape.1280, s32[64]{0:T(128)S(1)} %convert_add_fusion, s32[8,16]{1,0:T(8,128)S(1)} %multiply_add_fusion.5), kind=kOutput, calls=%fused_computation.251 | convolution fusion | flops 37756928 | bytes 295680 | tf_op jit(solution)/shard_map/dot_general | solution.py:138
  39.2 4.5 %all-to-all-start.1 = ((f32[8,16,384]{2,1,0:T(8,128)}), f32[8,16,384]{2,1,0:T(8,128)}, u32[]{:S(2)}, u32[]{:S(2)}) async-start(f32[8,16,384]{2,1,0:T(8,128)} %fusion.156), calls=%async_computation.1 | async-start | bytes 393216 | tf_op jit(solution)/shard_map/all_to_all | solution.py:146
  44.9 2.4 %copy.90 = f32[10,8,32,1]{3,2,1,0:T(8,128)} copy(f32[10,8,32,1]{2,1,3,0:T(8,128)} %collective-permute-done) | data formatting | bytes 20480 | tf_op jit(solution)/shard_map/ppermute | solution.py:38
  47.3 2.4 %copy.91 = f32[10,8,32,1]{3,2,1,0:T(8,128)} copy(f32[10,8,32,1]{2,1,3,0:T(8,128)} %collective-permute-done.1) | data formatting | bytes 20480 | tf_op jit(solution)/shard_map/ppermute | solution.py:41
  49.7 3.2 %pad_maximum_fusion = f32[10,8,32,130]{3,2,1,0:T(8,128)S(1)} fusion(f32[10,8,32,1]{3,2,1,0:T(8,128)} %copy.91, f32[10,8,32,128]{3,2,1,0:T(8,128)} %copy-done.9, f32[10,8,32,1]{3,2,1,0:T(8,128)} %copy.90), kind=kLoop, calls=%fused_computation.1 | loop fusion | flops 665600 | bytes 2662400 | tf_op jit(solution)/shard_map/concatenate | solution.py:42
  58.6 1.7 %collective-permute-start.2 = (f32[10,8,1,128]{3,1,2,0:T(8,128)S(1)}, f32[10,8,1,128]{3,1,2,0:T(8,128)S(1)}, u32[]{:S(2)}, u32[]{:S(2)}) collective-permute-start(f32[10,8,1,128]{3,1,2,0:T(8,128)S(1)} %copy.130), channel_id=1, source_target_pairs={{0,2},{2,4},{4,6},{6,0},{1,3},{3,5},{5,7},{7,1},{8,10},{10,12},{12... | collective-permute-start | bytes 122888 | tf_op jit(solution)/shard_map/ppermute | solution.py:38
  66.8 1.2 %collective-permute-start.5 = (f32[10,1,32,128]{3,2,1,0:T(8,128)}, f32[10,1,32,128]{3,2,1,0:T(8,128)}, u32[]{:S(2)}, u32[]{:S(2)}) collective-permute-start(f32[10,1,32,128]{3,2,1,0:T(8,128)} %get-tuple-element.55), channel_id=1, source_target_pairs={{1,0},{0,1},{3,2},{2,3},{5,4},{4,5},{7,6},{6,7},{9,8},{8,9},{11,10... | collective-permute-start | bytes 491528 | tf_op jit(solution)/shard_map/ppermute | solution.py:41
  69.6 1.1 %fusion.171 = f32[8,384]{1,0:T(8,128)S(1)} fusion(f32[128,384]{1,0:T(8,128)} %bitcast.53, f32[128]{0:T(128)S(1)} %eq.85), kind=kOutput, calls=%fused_computation.271 | convolution fusion | flops 4719616 | bytes 209408 | tf_op jit(solution)/shard_map/dot_general | solution.py:166
  70.8 3.1 %collective-permute-start.6 = (f32[3,128]{1,0:T(4,128)S(1)}, f32[3,128]{1,0:T(4,128)S(1)}, u32[]{:S(2)}, u32[]{:S(2)}) collective-permute-start(f32[3,128]{1,0:T(4,128)S(1)} %bitcast.225), channel_id=1, source_target_pairs={{0,1},{1,2},{2,3},{3,4},{4,5},{5,6},{6,7},{8,9},{9,10},{10,11},{11... | collective-permute-start | bytes 4616 | tf_op jit(solution)/shard_map/ppermute | solution.py:49
  73.8 1.6 %fusion.166 = f32[8,3,128]{2,1,0:T(4,128)S(1)} fusion(f32[8,128,128]{2,1,0:T(8,128)} %param.14, f32[8,3,128]{2,0,1:T(8,128)S(1)} %bitcast.221), kind=kOutput, calls=%fused_computation.263 | convolution fusion | flops 4718592 | bytes 548864 | tf_op jit(solution)/shard_map/skn,snm->skm/dot_general | solution.py:170
  75.4 1.3 %collective-permute-done.6 = f32[3,128]{1,0:T(4,128)S(1)} collective-permute-done((f32[3,128]{1,0:T(4,128)S(1)}, f32[3,128]{1,0:T(4,128)S(1)}, u32[]{:S(2)}, u32[]{:S(2)}) %collective-permute-start.6) | collective-permute-done | bytes 1568 | tf_op jit(solution)/shard_map/ppermute | solution.py:49
  78.3 1.7 %fusion.164 = f32[8,16,384]{2,1,0:T(8,128)} fusion(f32[8,384,1]{1,0,2:T(8,128)} %reshape.1281, f32[8,16]{1,0:T(8,128)} %bitcast.222), kind=kOutput, calls=%fused_computation.262 | convolution fusion | flops 4719616 | bytes 209408 | tf_op jit(solution)/shard_map/dot_general | solution.py:173
  80.6 4.0 %all-to-all-start.2 = ((f32[8,16,384]{2,1,0:T(8,128)}), f32[8,16,384]{2,1,0:T(8,128)}, u32[]{:S(2)}, u32[]{:S(2)}) async-start(f32[8,16,384]{2,1,0:T(8,128)} %fusion.164), calls=%async_computation.2 | async-start | bytes 393216 | tf_op jit(solution)/shard_map/all_to_all | solution.py:178
  84.6 1.4 %maximum_dynamic-update-slice_fusion.4 = f32[19,8,32,128]{3,2,1,0:T(8,128)} fusion(f32[19,8,32,128]{3,2,1,0:T(8,128)} %copy_dynamic-update-slice_fusion.4, f32[10,8,32,128]{3,2,1,0:T(8,128)S(1)} %copy_dynamic-update-slice_fusion.6, f32[10,1,32,128]{3,2,1,0:T(8,128)} %collective-permute-done.4), kind=kLoop, calls=%fused_computation.194 | loop fusion | flops 32768 | bytes 1605632
  86.0 1.4 %maximum_dynamic-update-slice_fusion.3 = f32[19,8,32,128]{3,2,1,0:T(8,128)} fusion(f32[19,8,32,128]{3,2,1,0:T(8,128)} %maximum_dynamic-update-slice_fusion.4, f32[10,1,32,128]{3,2,1,0:T(8,128)} %collective-permute-done.5, f32[10,8,32,128]{3,2,1,0:T(8,128)S(1)} %copy_dynamic-update-slice_fusion.6), kind=kLoop, calls=%fused_computation.193 | loop fusion | flops 32768 | bytes 1605632
  90.2 1.4 %maximum_dynamic-update-slice_fusion.2 = f32[19,8,32,128]{3,2,1,0:T(8,128)} fusion(f32[19,8,32,128]{3,2,1,0:T(8,128)} %copy_dynamic-update-slice_fusion, f32[10,8,32,128]{3,2,1,0:T(8,128)S(1)} %copy_dynamic-update-slice_fusion.6, f32[10,1,32,128]{3,2,1,0:T(8,128)} %collective-permute-done.4), kind=kLoop, calls=%fused_computation.188 | loop fusion | flops 32768 | bytes 1605632
  91.6 1.5 %maximum_dynamic-update-slice_fusion.1 = f32[19,8,32,128]{3,2,1,0:T(8,128)} fusion(f32[19,8,32,128]{3,2,1,0:T(8,128)} %maximum_dynamic-update-slice_fusion.2, f32[10,1,32,128]{3,2,1,0:T(8,128)} %collective-permute-done.5, f32[10,8,32,128]{3,2,1,0:T(8,128)S(1)} %copy_dynamic-update-slice_fusion.6), kind=kLoop, calls=%fused_computation.13 | loop fusion | flops 65536 | bytes 1736704
  93.1 1.5 %maximum_dynamic-update-slice_fusion = f32[19,8,32,128]{3,2,1,0:T(8,128)} fusion(f32[19,8,32,128]{3,2,1,0:T(8,128)} %maximum_dynamic-update-slice_fusion.1, f32[10,8,32,128]{3,2,1,0:T(8,128)S(1)} %copy_dynamic-update-slice_fusion.6, f32[10,1,32,128]{3,2,1,0:T(8,128)} %collective-permute-done.4), kind=kLoop, calls=%fused_computation.12 | loop fusion | flops 65536 | bytes 1736704
  94.5 1.5 %fusion.3 = f32[19,8,32,128]{3,2,1,0:T(8,128)} fusion(f32[19,8,32,128]{3,2,1,0:T(8,128)} %maximum_dynamic-update-slice_fusion, f32[10,1,32,128]{3,2,1,0:T(8,128)} %collective-permute-done.5, f32[10,8,32,128]{3,2,1,0:T(8,128)S(1)} %copy_dynamic-update-slice_fusion.6), kind=kLoop, calls=%fused_computation.11 | loop fusion | flops 65536 | bytes 1736704
  96.0 1.4 %fusion.137 = f32[19,8,32,128]{3,2,1,0:T(8,128)} fusion(f32[19,8,32,128]{3,2,1,0:T(8,128)} %fusion.3, f32[10,8,32,128]{3,2,1,0:T(8,128)S(1)} %copy_dynamic-update-slice_fusion.6, f32[10,1,32,128]{3,2,1,0:T(8,128)} %collective-permute-done.4), kind=kLoop, calls=%fused_computation.187 | loop fusion | flops 32768 | bytes 1605632 | tf_op jit(solution)/shard_map/stack | solution.py:114
  98.8 1.2 %fusion.151 = f32[64,3,128]{2,1,0:T(4,128)S(1)} fusion(bf16[64,128,128]{2,1,0:T(8,128)(2,1)S(1)} %copy-done, bf16[64,3,128]{2,0,1:T(8,128)(2,1)S(1)} %convolution_convert_fusion), kind=kOutput, calls=%fused_computation.243 | convolution fusion | flops 6291456 | bytes 2244608 | tf_op jit(solution)/shard_map/bks,bcs->bkc/dot_general | solution.py:189
  (128 shorter events, 31.1 us)
Async XLA Ops:
  0.6 32.8 %copy-start = (bf16[64,128,128]{2,1,0:T(8,128)(2,1)S(1)}, bf16[64,128,128]{2,1,0:T(8,128)(2,1)}, u32[]{:S(2)}) copy-start(bf16[64,128,128]{2,1,0:T(8,128)(2,1)} %param.11) | copy-start | bytes 6291460
  3.1 34.2 %copy-start.17 = (s32[64]{0:T(128)}, s32[64]{0:T(128)S(1)}, u32[]{:S(2)}) copy-start(s32[64]{0:T(128)S(1)} %convert_add_fusion) | copy-start | bytes 772
  4.7 34.5 %all-to-all-start = ((f32[8,1,16]{2,1,0:T(1,128)}), f32[8,1,16]{2,1,0:T(1,128)S(1)}, u32[]{:S(2)}, u32[]{:S(2)}) async-start(f32[8,1,16]{2,1,0:T(1,128)} %bitcast.50), calls=%async_computation | async-start | bytes 8192 | tf_op jit(solution)/shard_map/all_to_all | solution.py:153
  11.9 1.8 %copy-start.16 = (f32[4,19]{1,0:T(4,128)S(1)}, f32[4,19]{1,0:T(4,128)}, u32[]{:S(2)}) copy-start(f32[4,19]{1,0:T(4,128)} %constant.78.clone) | copy-start | bytes 916
  15.9 4.3 %copy-start.7 = (f32[1,32768]{1,0:T(1,128)}, f32[1,32768]{1,0:T(1,128)S(1)}, u32[]{:S(2)}) copy-start(f32[1,32768]{1,0:T(1,128)S(1)} %get-tuple-element.63) | copy-start | bytes 393220
  15.9 1.9 %copy-start.10 = (f32[19,8,32,128]{3,2,1,0:T(8,128)S(1)}, f32[19,8,32,128]{3,2,1,0:T(8,128)}, u32[]{:S(2)}) copy-start(f32[19,8,32,128]{3,2,1,0:T(8,128)} %param.10) | copy-start | bytes 7471108
  17.2 3.0 %copy-start.1 = (f32[1,32768]{1,0:T(1,128)}, f32[1,32768]{1,0:T(1,128)S(1)}, u32[]{:S(2)}) copy-start(f32[1,32768]{1,0:T(1,128)S(1)} %get-tuple-element.69) | copy-start | bytes 393220
  17.2 3.0 %copy-start.3 = (f32[1,32768]{1,0:T(1,128)}, f32[1,32768]{1,0:T(1,128)S(1)}, u32[]{:S(2)}) copy-start(f32[1,32768]{1,0:T(1,128)S(1)} %get-tuple-element.68) | copy-start | bytes 393220
  17.9 2.3 %copy-start.5 = (f32[1,8,32,128]{3,2,1,0:T(8,128)}, f32[1,8,32,128]{3,2,1,0:T(8,128)S(1)}, u32[]{:S(2)}) copy-start(f32[1,8,32,128]{3,2,1,0:T(8,128)S(1)} %get-tuple-element.28) | copy-start | bytes 393220
  20.3 2.0 %copy-start.9 = (f32[10,8,32,128]{3,2,1,0:T(8,128)}, f32[10,8,32,128]{3,2,1,0:T(8,128)S(1)}, u32[]{:S(2)}) copy-start(f32[10,8,32,128]{3,2,1,0:T(8,128)S(1)} %fusion.80) | copy-start | bytes 3932164
  22.3 8.3 %copy-start.19 = (s32[64]{0:T(128)S(1)}, s32[64]{0:T(128)}, u32[]{:S(2)}) copy-start(s32[64]{0:T(128)} %param.16) | copy-start | bytes 772
  24.8 22.5 %collective-permute-start.1 = (f32[10,8,32,1]{2,1,3,0:T(8,128)}, f32[10,8,32,1]{2,1,3,0:T(8,128)}, u32[]{:S(2)}, u32[]{:S(2)}) collective-permute-start(f32[10,8,32,1]{2,1,3,0:T(8,128)} %copy.113), channel_id=1, source_target_pairs={{8,0},{16,8},{24,16},{0,24},{9,1},{17,9},{25,17},{1,25},{10,2},{18... | collective-permute-start | bytes 30728 | tf_op jit(solution)/shard_map/ppermute | solution.py:41
  30.6 14.4 %collective-permute-start = (f32[10,8,32,1]{2,1,3,0:T(8,128)}, f32[10,8,32,1]{2,1,3,0:T(8,128)}, u32[]{:S(2)}, u32[]{:S(2)}) collective-permute-start(f32[10,8,32,1]{2,1,3,0:T(8,128)} %copy.112), channel_id=1, source_target_pairs={{0,8},{8,16},{16,24},{24,0},{1,9},{9,17},{17,25},{25,1},{2,10},{10... | collective-permute-start | bytes 30728 | tf_op jit(solution)/shard_map/ppermute | solution.py:38
  39.2 10.6 %copy-start.15 = (f32[8,1,16]{2,1,0:T(1,128)}, f32[8,1,16]{2,1,0:T(1,128)S(1)}, u32[]{:S(2)}) copy-start(f32[8,1,16]{2,1,0:T(1,128)S(1)} %all-to-all-done) | copy-start | bytes 1540
  39.2 30.5 %all-to-all-start.1 = ((f32[8,16,384]{2,1,0:T(8,128)}), f32[8,16,384]{2,1,0:T(8,128)}, u32[]{:S(2)}, u32[]{:S(2)}) async-start(f32[8,16,384]{2,1,0:T(8,128)} %fusion.156), calls=%async_computation.1 | async-start | bytes 393216 | tf_op jit(solution)/shard_map/all_to_all | solution.py:146
  52.9 1.3 %copy-start.11 = (f32[10,8,32,128]{3,2,1,0:T(8,128)S(1)}, f32[10,8,32,128]{3,2,1,0:T(8,128)}, u32[]{:S(2)}) copy-start(f32[10,8,32,128]{3,2,1,0:T(8,128)} %get-tuple-element.30) | copy-start | bytes 3932164
  53.1 1.3 %copy-start.2 = (f32[1,32768]{1,0:T(1,128)S(1)}, f32[1,32768]{1,0:T(1,128)}, u32[]{:S(2)}) copy-start(f32[1,32768]{1,0:T(1,128)} %copy-done.1) | copy-start | bytes 393220
  53.2 1.3 %copy-start.4 = (f32[1,32768]{1,0:T(1,128)S(1)}, f32[1,32768]{1,0:T(1,128)}, u32[]{:S(2)}) copy-start(f32[1,32768]{1,0:T(1,128)} %copy-done.3) | copy-start | bytes 393220
  53.2 1.3 %copy-start.6 = (f32[1,8,32,128]{3,2,1,0:T(8,128)S(1)}, f32[1,8,32,128]{3,2,1,0:T(8,128)}, u32[]{:S(2)}) copy-start(f32[1,8,32,128]{3,2,1,0:T(8,128)} %copy-done.5) | copy-start | bytes 393220
  53.2 1.3 %copy-start.8 = (f32[1,32768]{1,0:T(1,128)S(1)}, f32[1,32768]{1,0:T(1,128)}, u32[]{:S(2)}) copy-start(f32[1,32768]{1,0:T(1,128)} %copy-done.7) | copy-start | bytes 393220
  58.6 3.4 %collective-permute-start.2 = (f32[10,8,1,128]{3,1,2,0:T(8,128)S(1)}, f32[10,8,1,128]{3,1,2,0:T(8,128)S(1)}, u32[]{:S(2)}, u32[]{:S(2)}) collective-permute-start(f32[10,8,1,128]{3,1,2,0:T(8,128)S(1)} %copy.130), channel_id=1, source_target_pairs={{0,2},{2,4},{4,6},{6,0},{1,3},{3,5},{5,7},{7,1},{8,10},{10,12},{12... | collective-permute-start | bytes 122888 | tf_op jit(solution)/shard_map/ppermute | solution.py:38
  60.3 3.4 %collective-permute-start.3 = (f32[10,8,1,128]{3,1,2,0:T(8,128)S(1)}, f32[10,8,1,128]{3,1,2,0:T(8,128)S(1)}, u32[]{:S(2)}, u32[]{:S(2)}) collective-permute-start(f32[10,8,1,128]{3,1,2,0:T(8,128)S(1)} %copy.131), channel_id=1, source_target_pairs={{2,0},{4,2},{6,4},{0,6},{3,1},{5,3},{7,5},{1,7},{10,8},{12,10},{14... | collective-permute-start | bytes 122888 | tf_op jit(solution)/shard_map/ppermute | solution.py:41
  66.8 19.2 %collective-permute-start.5 = (f32[10,1,32,128]{3,2,1,0:T(8,128)}, f32[10,1,32,128]{3,2,1,0:T(8,128)}, u32[]{:S(2)}, u32[]{:S(2)}) collective-permute-start(f32[10,1,32,128]{3,2,1,0:T(8,128)} %get-tuple-element.55), channel_id=1, source_target_pairs={{1,0},{0,1},{3,2},{2,3},{5,4},{4,5},{7,6},{6,7},{9,8},{8,9},{11,10... | collective-permute-start | bytes 491528 | tf_op jit(solution)/shard_map/ppermute | solution.py:41
  68.0 16.6 %collective-permute-start.4 = (f32[10,1,32,128]{3,2,1,0:T(8,128)}, f32[10,1,32,128]{3,2,1,0:T(8,128)}, u32[]{:S(2)}, u32[]{:S(2)}) collective-permute-start(f32[10,1,32,128]{3,2,1,0:T(8,128)} %get-tuple-element.56), channel_id=1, source_target_pairs={{0,1},{1,0},{2,3},{3,2},{4,5},{5,4},{6,7},{7,6},{8,9},{9,8},{10,11... | collective-permute-start | bytes 491528 | tf_op jit(solution)/shard_map/ppermute | solution.py:38
  70.8 5.9 %collective-permute-start.6 = (f32[3,128]{1,0:T(4,128)S(1)}, f32[3,128]{1,0:T(4,128)S(1)}, u32[]{:S(2)}, u32[]{:S(2)}) collective-permute-start(f32[3,128]{1,0:T(4,128)S(1)} %bitcast.225), channel_id=1, source_target_pairs={{0,1},{1,2},{2,3},{3,4},{4,5},{5,6},{6,7},{8,9},{9,10},{10,11},{11... | collective-permute-start | bytes 4616 | tf_op jit(solution)/shard_map/ppermute | solution.py:49
  80.6 16.8 %all-to-all-start.2 = ((f32[8,16,384]{2,1,0:T(8,128)}), f32[8,16,384]{2,1,0:T(8,128)}, u32[]{:S(2)}, u32[]{:S(2)}) async-start(f32[8,16,384]{2,1,0:T(8,128)} %fusion.164), calls=%async_computation.2 | async-start | bytes 393216 | tf_op jit(solution)/shard_map/all_to_all | solution.py:178
  84.6 2.9 %copy-start.14 = (f32[1,8,32,128]{3,1,2,0:T(8,128)S(1)}, f32[1,8,32,128]{3,1,2,0:T(8,128)}, u32[]{:S(2)}) copy-start(f32[1,8,32,128]{3,1,2,0:T(8,128)} %slice_bitcast_fusion.24) | copy-start | bytes 393220
  86.0 2.1 %copy-start.13 = (f32[1,8,32,128]{3,1,2,0:T(8,128)S(1)}, f32[1,8,32,128]{3,1,2,0:T(8,128)}, u32[]{:S(2)}) copy-start(f32[1,8,32,128]{3,1,2,0:T(8,128)} %slice_bitcast_fusion.23) | copy-start | bytes 393220
  86.0 2.8 %copy-start.12 = (f32[1,8,32,128]{3,1,2,0:T(8,128)S(1)}, f32[1,8,32,128]{3,1,2,0:T(8,128)}, u32[]{:S(2)}) copy-start(f32[1,8,32,128]{3,1,2,0:T(8,128)} %slice_bitcast_fusion.22) | copy-start | bytes 393220
  96.0 2.4 %copy-start.18 = (s32[64]{0:T(128)S(1)}, s32[64]{0:T(128)}, u32[]{:S(2)}) copy-start(s32[64]{0:T(128)} %copy-done.17) | copy-start | bytes 772
where the time goes:
time: 102 us; the launch traced here: 101 us
  local copies, waits for them, and re-layouts  35.7 us (35%)
  other arithmetic  24.6 us (24%)
  starting transfers between devices  23.2 us (23%)
  matrix products  13.6 us (13%)
  waiting for transfers between devices  2.22 us (2%)
  between operations  1.2 us (1%)
    unnamed x68, local copies, waits for them, and re-layouts  18.6 us
    unnamed x19, other arithmetic  13.9 us
    all_to_all x1, starting transfers between devices, body(): lax.all_to_all(outgoing_tags.reshape(owner_count, capacity), ('gy', 'gz')...  5.22 us
    all_to_all x1, starting transfers between devices, body(): lax.all_to_all(outgoing.reshape(owner_count, capacity, 3 * node_count), (...  4.48 us
    ppermute x3, starting transfers between devices, padded_2(): lax.ppermute(lax.slice_in_dim(block, 0, width, axis=dim), axis, backward)  4.48 us
    all_to_all x1, starting transfers between devices, body(): lax.all_to_all(returned.reshape(owner_count, capacity, 3 * node_count), (...  3.97 us
    concatenate x1, other arithmetic, padded_2(): block = jnp.concatenate([low, block, high], axis=dim)  3.18 us
    ppermute x1, starting transfers between devices, from_behind(): return lax.ppermute(array, axis, pairs)  3.06 us
  transfers between devices with their start and end apart: 10, of which 2 were waited for; matrix products, arithmetic and copies ran while one was open for 65% of the time, Pallas kernels for 0%

commit v1 on v0

v1 whole, which is shorter than its diff:
```python
import functools

import jax
import jax.numpy as jnp
from jax import lax
from jax.experimental import pallas as pl
from jax.experimental.pallas import tpu as pltpu
from jax.sharding import PartitionSpec as P

MESH = pl.DeviceIdType.MESH
F32 = jnp.float32
BF16 = jnp.bfloat16
I32 = jnp.int32

lattice_velocity = (
    (0, 0, 0),
    (1, 0, 0),
    (-1, 0, 0),
    (0, 1, 0),
    (0, -1, 0),
    (0, 0, 1),
    (0, 0, -1),
    (1, 1, 0),
    (-1, -1, 0),
    (1, -1, 0),
    (-1, 1, 0),
    (1, 0, 1),
    (-1, 0, -1),
    (1, 0, -1),
    (-1, 0, 1),
    (0, 1, 1),
    (0, -1, -1),
    (0, 1, -1),
    (0, -1, 1),
)
lattice_weight = (1.0 / 3.0,) + (1.0 / 18.0,) * 6 + (1.0 / 36.0,) * 12
load_scale = 30.0
relaxation = 1.6


def moving(component, sign):
    return [q for q in range(19) if lattice_velocity[q][component] == sign]


XP, XM = moving(0, 1), moving(0, -1)
YP, YM = moving(1, 1), moving(1, -1)
ZP, ZM = moving(2, 1), moving(2, -1)
NOT_Z = [q for q in range(19) if lattice_velocity[q][2] == 0]


def iota(shape, dim):
    return lax.broadcasted_iota(I32, shape, dim)


def split(value):
    high = value.astype(BF16)
    low = (value - high.astype(F32)).astype(BF16)
    return high, low


def dot(a, b):
    return jnp.dot(a, b, preferred_element_type=F32)


def kernel(
    sizes,
    pop, rbf, owner, slot, comp, ncomp, row,
    out, disp, wall,
    f, moments, grid, mom, weights, compliance, coupling,
    gather, place, spread, traction, forces, part, recv, mine, shells,
    xs, xr, ys, yr, zr,
    in_sem, w_sem, ps_sem, pr_sem, ds_sem, dr_sem, hs_sem, hr_sem, zs_sem, zr_sem, o_sem,
):
    gxn, gyn, gzn = sizes
    owners = gyn * gzn
    depth, height, width = grid.shape[1:]
    blocks = weights.shape[0]
    shell = compliance.shape[0]
    rows8 = blocks * 8
    cells = depth * height
    gx, gy, gz = lax.axis_index("gx"), lax.axis_index("gy"), lax.axis_index("gz")
    me = gy * gzn + gz

    def peer(index):
        return (gx, index // gzn, index % gzn)

    def step(a, n, by):
        return lax.rem(a + by + n, n)

    right = (step(gx, gxn, 1), gy, gz)
    left = (step(gx, gxn, -1), gy, gz)
    north = (gx, step(gy, gyn, 1), gz)
    south = (gx, step(gy, gyn, -1), gz)
    up = (gx, gy, step(gz, gzn, 1))
    down = (gx, gy, step(gz, gzn, -1))

    loads_in = [pltpu.make_async_copy(pop.at[:, z], f.at[:, z], in_sem.at[z]) for z in range(depth)]
    for copy in loads_in:
        copy.start()
    fixed = [
        pltpu.make_async_copy(rbf, weights, w_sem.at[0]),
        pltpu.make_async_copy(comp, compliance, w_sem.at[1]),
        pltpu.make_async_copy(ncomp, coupling, w_sem.at[2]),
    ]
    for copy in fixed:
        copy.start()

    barrier = pltpu.get_barrier_semaphore()

    def greet(d, carry):
        pl.semaphore_signal(
            barrier, inc=1, device_id=peer(lax.rem(me + d, owners)), device_id_type=MESH
        )
        return carry

    lax.fori_loop(1, owners, greet, 0)
    for item in (left, right):
        pl.semaphore_signal(barrier, inc=1, device_id=item, device_id_type=MESH)

    square = iota((blocks, blocks), 0) == iota((blocks, blocks), 1)

    def down_rows(ref):
        return jnp.sum(jnp.where(square, ref[...], 0).astype(F32), axis=1, keepdims=True)

    row_s, owner_s, slot_s = down_rows(row), down_rows(owner), down_rows(slot)
    wide = jnp.concatenate(
        [jnp.broadcast_to(item, (blocks, 128)) for item in (row_s, owner_s, slot_s)], axis=1
    ).astype(BF16)
    repeat = (iota((rows8, blocks), 0) // 8 == iota((rows8, blocks), 1)).astype(F32).astype(BF16)
    tall = dot(repeat, wide).astype(I32)
    kind = iota((rows8, 128), 0) % 8
    row_key = tall[:, :128] + kind * cells
    lane = iota((rows8, 128), 1)
    for j in range(3 * cells // 128):
        hit = row_key == lane + 128 * j
        gather[:, j * 128 : (j + 1) * 128] = hit.astype(F32).astype(BF16)
    target_key = (tall[:, 128:256] * shell + tall[:, 256:]) * 3 + kind
    target_key = jnp.where(kind < 3, target_key, -2)
    for j in range(owners * 32 // 128):
        column = lane + 128 * j
        column_key = jnp.where(column % 32 < 3 * shell, column // 32 * (3 * shell) + column % 32, -1)
        spread[:, j * 128 : (j + 1) * 128] = (target_key == column_key).astype(F32).astype(BF16)
    target_s = ((owner_s * shell + slot_s) * 3).astype(I32)
    across = iota((blocks, rows8), 1)
    lane_key = jnp.sum(
        jnp.where(across // 8 == iota((blocks, rows8), 0), target_s, 0).astype(F32),
        axis=0, keepdims=True,
    ).astype(I32)
    lane_kind = iota((1, rows8), 1) % 8
    lane_key = jnp.where(lane_kind < 3, lane_key + lane_kind, -100)
    place_row = iota((owners * 32, rows8), 0)
    place_key = jnp.where(
        place_row % 32 < 3 * shell + 3,
        place_row // 32 * (3 * shell) - 3 + place_row % 32,
        -1000,
    )
    place[...] = (place_key == lane_key).astype(F32).astype(BF16)

    for z in range(depth):
        loads_in[z].wait()

        def moment(c, carry, z=z):
            at = pl.ds(pl.multiple_of(c * 16, 16), 16)
            v = [f[q, z, at, :] for q in range(19)]
            total = v[0]
            for q in range(1, 19):
                total = total + v[q]
            moments[0, z, at, :] = total
            for k in range(3):
                plus, minus = moving(k, 1), moving(k, -1)
                a, b = v[plus[0]], v[minus[0]]
                for q in plus[1:]:
                    a = a + v[q]
                for q in minus[1:]:
                    b = b + v[q]
                m = a - b
                moments[1 + k, z, at, :] = m
                here = pl.ds(pl.multiple_of(k * cells + z * height + c * 16, 16), 16)
                mom[here, :] = (load_scale * m).astype(BF16)
            return carry

        for c in range(height // 16):
            moment(c, 0)

    traction[...] = dot(gather[...], mom[...])
    fixed[0].wait()

    def force(g, carry):
        for i in range(8):
            at = pl.ds(pl.multiple_of(g * 64 + i * 8, 8), 8)
            forces[at, :] = dot(traction[at, :].astype(BF16), weights[g * 8 + i])
        return carry

    lax.fori_loop(0, blocks // 8, force, 0)
    high, low = split(forces[...])
    both = dot(place[...], jnp.concatenate([high, low], axis=1))
    part[...] = (both[:, :128] + both[:, 128:]).reshape(owners, 32, 128)
    pl.semaphore_wait(barrier, owners - 1 + 2)

    def part_copy(other, mine_at):
        return pltpu.make_async_remote_copy(
            src_ref=part.at[other], dst_ref=recv.at[mine_at],
            send_sem=ps_sem.at[other], recv_sem=pr_sem.at[mine_at],
            device_id=peer(other), device_id_type=MESH,
        )

    def send_part(d, carry):
        part_copy(lax.rem(me + d, owners), me).start()
        return carry

    lax.fori_loop(1, owners, send_part, 0)

    lanes = iota((16, width), 1)

    def collide(z, carry):
        for c in range(height // 16):
            at = pl.ds(c * 16, 16)
            rho = moments[0, z, at, :]
            inverse = 1.0 / rho
            u = [moments[1 + k, z, at, :] * inverse for k in range(3)]
            base = 1.0 - 1.5 * (u[0] * u[0] + u[1] * u[1] + u[2] * u[2])
            scaled = [relaxation * w * rho for w in (1 / 3.0, 1 / 18.0, 1 / 36.0)]
            result = [None] * 19
            result[0] = (1.0 - relaxation) * f[0, z, at, :] + scaled[0] * base
            for q in range(1, 19, 2):
                p = None
                for k in range(3):
                    s = lattice_velocity[q][k]
                    if s:
                        term = u[k]
                        p = (term if s > 0 else -term) if p is None else (p + term if s > 0 else p - term)
                w = scaled[1] if q < 7 else scaled[2]
                even = w * (base + 4.5 * (p * p))
                odd = w * (3.0 * p)
                result[q] = (1.0 - relaxation) * f[q, z, at, :] + (even + odd)
                result[q + 1] = (1.0 - relaxation) * f[q + 1, z, at, :] + (even - odd)
            sent = [xs[0, at, :], xs[1, at, :]]
            for d in range(5):
                here = lanes == d * depth + z
                sent[0] = jnp.where(here, result[XP[d]][:, width - 1 :], sent[0])
                sent[1] = jnp.where(here, result[XM[d]][:, :1], sent[1])
                result[XP[d]] = pltpu.roll(result[XP[d]], 1, 1)
                result[XM[d]] = pltpu.roll(result[XM[d]], width - 1, 1)
            xs[0, at, :] = sent[0]
            xs[1, at, :] = sent[1]
            for q in range(19):
                grid[q, z, at, :] = result[q]
        return carry

    xs[...] = jnp.zeros_like(xs)
    lax.fori_loop(0, depth, collide, 0)

    def halo(src, dst, number, device):
        return pltpu.make_async_remote_copy(
            src_ref=src, dst_ref=dst, send_sem=hs_sem.at[number], recv_sem=hr_sem.at[number],
            device_id=device, device_id_type=MESH,
        )

    x_copies = [halo(xs.at[0], xr.at[0], 0, right), halo(xs.at[1], xr.at[1], 1, left)]
    for copy in x_copies:
        copy.start()

    fixed[1].wait()
    fixed[2].wait()
    comp_high, comp_low = split(compliance[...])
    coup_high, coup_low = split(coupling[...])

    def take_part(d, total):
        other = lax.rem(me + d, owners)
        part_copy(me, other).wait_recv()
        return total + recv[other]

    load = lax.fori_loop(1, owners, take_part, part[me])
    load_high, load_low = split(load)
    aligned = 8 * (shell + 1)
    r8, c8 = iota((aligned, 32), 0), iota((aligned, 32), 1)
    expand = ((r8 % 8 < 3) & (r8 // 8 * 3 + r8 % 8 == c8)).astype(F32).astype(BF16)
    tall_load = dot(expand, jnp.concatenate([load_high, load_low], axis=1))
    moved = []
    for s in range(shell + 1):
        hi = tall_load[s * 8 : s * 8 + 8, :128]
        lo = tall_load[s * 8 : s * 8 + 8, 128:]
        pair = jnp.concatenate([hi, lo], axis=0).astype(BF16)
        first = comp_high[s - 1] if s else coup_high
        second = comp_low[s - 1] if s else coup_low
        a = dot(pair, first)
        b = dot(pair, second)
        moved.append(a[:8] + a[8:] + b[:8])
    moved[1] = moved[1] + moved[0]
    for s in range(shell):
        disp[s] = moved[s + 1][:3]
    r8, c8 = iota((32, 8 * shell), 0), iota((32, 8 * shell), 1)
    compact = ((c8 % 8 < 3) & (c8 // 8 * 3 + c8 % 8 == r8)).astype(F32).astype(BF16)
    rounded = jnp.concatenate(moved[1:], axis=0).astype(BF16)
    own = dot(compact, rounded)
    mine[...] = own
    shells[me] = own

    def disp_copy(other, at):
        return pltpu.make_async_remote_copy(
            src_ref=mine, dst_ref=shells.at[at],
            send_sem=ds_sem.at[other], recv_sem=dr_sem.at[at],
            device_id=peer(other), device_id_type=MESH,
        )

    def send_disp(d, carry):
        disp_copy(lax.rem(me + d, owners), me).start()
        return carry

    lax.fori_loop(1, owners, send_disp, 0)

    for copy in x_copies:
        copy.wait_recv()
    for d in range(5):
        for z in range(depth):
            i = d * depth + z
            grid[XP[d], z, :, 0:1] = xr[0, :, i : i + 1]
            grid[XM[d], z, :, width - 1 :] = xr[1, :, i : i + 1]
    for d in range(5):
        ys[0, d] = grid[YP[d], :, height - 1, :]
        ys[1, d] = grid[YM[d], :, 0, :]
    y_copies = [halo(ys.at[0], yr.at[0], 2, north), halo(ys.at[1], yr.at[1], 3, south)]
    for copy in y_copies:
        copy.start()
    ylane = iota((height, width), 0)

    for copy in y_copies:
        copy.wait_recv()

    def shift_y(z, carry):
        for d in range(5):
            q = YP[d]
            grid[q, z] = jnp.where(ylane == 0, yr[0, d, pl.ds(z, 1), :], pltpu.roll(grid[q, z], 1, 0))
            q = YM[d]
            grid[q, z] = jnp.where(
                ylane == height - 1, yr[1, d, pl.ds(z, 1), :], pltpu.roll(grid[q, z], height - 1, 0)
            )
        return carry

    lax.fori_loop(0, depth, shift_y, 0)
    z_copies = []
    for d in range(5):
        for side, q, z, device in ((0, ZP[d], depth - 1, up), (1, ZM[d], 0, down)):
            z_copies.append(
                pltpu.make_async_remote_copy(
                    src_ref=grid.at[q, z], dst_ref=zr.at[side, d],
                    send_sem=zs_sem.at[side, d], recv_sem=zr_sem.at[side, d],
                    device_id=device, device_id_type=MESH,
                )
            )
            z_copies[-1].start()
    written = []

    def write(src, dst):
        written.append(pltpu.make_async_copy(src, dst, o_sem.at[len(written)]))
        written[-1].start()

    for q in NOT_Z:
        write(grid.at[q], out.at[q])
    for d in range(5):
        write(grid.at[ZP[d], 0 : depth - 1], out.at[ZP[d], 1:depth])
        write(grid.at[ZM[d], 1:depth], out.at[ZM[d], 0 : depth - 1])

    def take_disp(d, carry):
        other = lax.rem(me + d, owners)
        disp_copy(other, other).wait_recv()
        return carry

    lax.fori_loop(1, owners, take_disp, 0)
    everything = shells[...].reshape(owners * 32, 128).astype(BF16)
    traction[...] = dot(spread[...], everything)

    def motion(g, carry):
        for i in range(8):
            at = pl.ds(pl.multiple_of(g * 64 + i * 8, 8), 8)
            value = lax.dot_general(
                traction[at, :].astype(BF16), weights[g * 8 + i],
                (((1,), (1,)), ((), ())), preferred_element_type=F32,
            )
            wall[g * 8 + i] = value[:3]
        return carry

    lax.fori_loop(0, blocks // 8, motion, 0)

    for copy in z_copies:
        copy.wait_recv()
    for d in range(5):
        write(zr.at[0, d], out.at[ZP[d], 0])
        write(zr.at[1, d], out.at[ZM[d], depth - 1])

    def drain(d, carry):
        other = lax.rem(me + d, owners)
        part_copy(other, me).wait_send()
        disp_copy(other, me).wait_send()
        return carry

    lax.fori_loop(1, owners, drain, 0)
    for copy in x_copies + y_copies + z_copies:
        copy.wait_send()
    for copy in written:
        copy.wait()


def body(sizes, pop, rbf, owner, slot, comp, ncomp, row):
    _, depth, height, width = pop.shape
    blocks, _, nodes = rbf.shape
    shell = comp.shape[0]
    owners = sizes[1] * sizes[2]
    rows8 = blocks * 8
    any_space = pl.BlockSpec(memory_space=pl.ANY)
    vmem = pl.BlockSpec(memory_space=pltpu.VMEM)
    dma = pltpu.SemaphoreType.DMA
    return pl.pallas_call(
        functools.partial(kernel, sizes),
        out_shape=(
            jax.ShapeDtypeStruct(pop.shape, F32),
            jax.ShapeDtypeStruct((shell, 3, nodes), F32),
            jax.ShapeDtypeStruct((blocks, 3, width), F32),
        ),
        in_specs=[any_space, any_space, vmem, vmem, any_space, any_space, vmem],
        out_specs=(any_space, vmem, vmem),
        scratch_shapes=[
            pltpu.VMEM(pop.shape, F32),
            pltpu.VMEM((4, depth, height, width), F32),
            pltpu.VMEM(pop.shape, F32),
            pltpu.VMEM((3 * depth * height, width), BF16),
            pltpu.VMEM(rbf.shape, BF16),
            pltpu.VMEM(comp.shape, F32),
            pltpu.VMEM(ncomp.shape, F32),
            pltpu.VMEM((rows8, 3 * depth * height), BF16),
            pltpu.VMEM((owners * 32, rows8), BF16),
            pltpu.VMEM((rows8, owners * 32), BF16),
            pltpu.VMEM((rows8, 128), F32),
            pltpu.VMEM((rows8, 128), F32),
            pltpu.VMEM((owners, 32, 128), F32),
            pltpu.VMEM((owners, 32, 128), F32),
            pltpu.VMEM((32, 128), F32),
            pltpu.VMEM((owners, 32, 128), F32),
            pltpu.VMEM((2, height, 128), F32),
            pltpu.VMEM((2, height, 128), F32),
            pltpu.VMEM((2, 5, depth, width), F32),
            pltpu.VMEM((2, 5, depth, width), F32),
            pltpu.VMEM((2, 5, height, width), F32),
            dma((depth,)),
            dma((3,)),
            dma((owners,)),
            dma((owners,)),
            dma((owners,)),
            dma((owners,)),
            dma((4,)),
            dma((4,)),
            dma((2, 5)),
            dma((2, 5)),
            dma((len(NOT_Z) + 20,)),
        ],
        compiler_params=pltpu.CompilerParams(
            collective_id=0, has_side_effects=True, vmem_limit_bytes=48 * 1024 * 1024
        ),
        name="wind_roof_step",
    )(
        pop, rbf, owner.reshape(1, blocks), slot.reshape(1, blocks), comp, ncomp,
        row.reshape(1, blocks),
    )


def solution(mesh):
    sizes = tuple(mesh.shape[name] for name in ("gx", "gy", "gz"))
    return jax.shard_map(
        functools.partial(body, sizes),
        mesh=mesh,
        in_specs=(
            P(None, "gz", "gy", "gx"),
            P(("gx", "gy", "gz"), None, None),
            P(("gx", "gy", "gz"), None),
            P(("gx", "gy", "gz"), None),
            P(("gx", "gy", "gz"), None, None),
            P(("gx", "gy", "gz"), None),
            P(("gx", "gy", "gz")),
        ),
        out_specs=(
            P(None, "gz", "gy", "gx"),
            P(("gx", "gy", "gz"), None, None),
            P(("gx", "gy", "gz"), None, None),
        ),
        check_vma=False,
    )
```

time: 102 us -> 31.9 us (0.31); the launches traced: 101 us -> 31.6 us
  local copies, waits for them, and re-layouts: 35.7 us -> 8.13 us
  other arithmetic: 24.6 us -> 0 us
  starting transfers between devices: 23.2 us -> 0 us
  Pallas kernels: 0 us -> 22.8 us
  matrix products: 13.6 us -> 0 us
  waiting for transfers between devices: 2.22 us -> 0 us
    pallas_call x0 -> x1, Pallas kernels: none -> 22.8 us  [body(): pl.pallas_call(functools.partial(kernel, sizes), out_shape=(jax.ShapeDtyp...]
    unnamed x19 -> x0, other arithmetic: 13.9 us -> none
    all_to_all x3 -> x0, starting transfers between devices: 13.7 us -> none  [the longest x1 5.22 us: body(): lax.all_to_all(outgoing_tags.reshape(owner_count, capacity), ('gy', 'gz')...]
    dot_general x10 -> x0, matrix products: 13.6 us -> none  [the longest x1 2.27 us: body(): jnp.einsum('kbc,bcs->bks', traction, rbf_weights, preferred_element_type=...]
    unnamed x68 -> x13, local copies, waits for them, and re-layouts: 18.6 us -> 6.88 us
    ppermute x7 -> x0, starting transfers between devices: 9.56 us -> none  [the longest x3 4.48 us: padded_2(): lax.ppermute(lax.slice_in_dim(block, 0, width, axis=dim), axis, backward)]
    ppermute x2 -> x0, local copies, waits for them, and re-layouts: 4.8 us -> none  [the longest x1 2.41 us: padded_2(): lax.ppermute(lax.slice_in_dim(block, 0, width, axis=dim), axis, backward)]
    reshape x3 -> x0, local copies, waits for them, and re-layouts: 3.28 us -> none  [the longest x1 1.6 us: body(): forces = forces.reshape(block_count, 3 * node_count)]
  transfers between devices with their start and end apart: 10 -> 0, of which waited for: 2 -> 0; matrix products, arithmetic and copies ran while one was open for 65% -> 0% of each run, Pallas kernels for 0% -> 0%
where the time goes in v1:
time: 31.9 us; the launch traced here: 31.6 us
  Pallas kernels  22.8 us (71%)
  local copies, waits for them, and re-layouts  8.13 us (25%)
  between operations  0.66 us (2%)
    pallas_call x1, Pallas kernels, body(): pl.pallas_call(functools.partial(kernel, sizes), out_shape=(jax.ShapeDtyp...  22.8 us
    unnamed x13, local copies, waits for them, and re-layouts  6.88 us
    pallas_call x2, local copies, waits for them, and re-layouts, body(): pl.pallas_call(functools.partial(kernel, sizes), out_shape=(jax.ShapeDtyp...  1.25 us

profile of v1, /device:TPU:1, one launch (start us, length us, event | category | flops | bytes accessed | tf_op | source)
XLA Modules:
  0.0 31.6 jit_solution(4394979952586585725)
XLA Ops:
  0.6 0.0 copy-start
  0.6 1.6 %copy-done = bf16[64,128,128]{2,1,0:T(8,128)(2,1)S(1)} copy-done((bf16[64,128,128]{2,1,0:T(8,128)(2,1)S(1)}, bf16[64,128,128]{2,1,0:T(8,128)(2,1)}, u32[]{:S(2)}) %copy-start) | copy-done | bytes 2097176
  2.2 0.0 copy-start.1
  2.2 1.0 %copy-done.1 = f32[8,128,128]{2,1,0:T(8,128)S(1)} copy-done((f32[8,128,128]{2,1,0:T(8,128)S(1)}, f32[8,128,128]{2,1,0:T(8,128)}, u32[]{:S(2)}) %copy-start.1) | copy-done | bytes 524312
  3.3 0.0 copy-start.2
  3.3 0.8 %copy-done.2 = f32[128,128]{1,0:T(8,128)S(1)} copy-done((f32[128,128]{1,0:T(8,128)S(1)}, f32[128,128]{1,0:T(8,128)}, u32[]{:S(2)}) %copy-start.2) | copy-done | bytes 65560
  4.1 0.0 copy-start.3
  4.1 0.7 %copy-done.3 = s32[64,1]{0,1:T(1,128)S(1)} copy-done((s32[64,1]{0,1:T(1,128)S(1)}, s32[64,1]{0,1:T(1,128)}, u32[]{:S(2)}) %copy-start.3) | copy-done | bytes 280
  4.8 0.0 copy-start.4
  4.8 0.7 %copy-done.4 = s32[64,1]{0,1:T(1,128)S(1)} copy-done((s32[64,1]{0,1:T(1,128)S(1)}, s32[64,1]{0,1:T(1,128)}, u32[]{:S(2)}) %copy-start.4) | copy-done | bytes 280
  5.4 0.0 copy-start.5
  5.4 0.7 %copy-done.5 = s32[64]{0:T(128)S(1)} copy-done((s32[64]{0:T(128)S(1)}, s32[64]{0:T(128)}, u32[]{:S(2)}) %copy-start.5) | copy-done | bytes 280
  6.1 22.8 %wind_roof_step.1 = (f32[19,8,32,128]{3,2,1,0:T(8,128)S(1)}, f32[8,3,128]{2,1,0:T(4,128)S(1)}, f32[64,3,128]{2,1,0:T(4,128)S(1)}) custom-call(f32[19,8,32,128]{3,2,1,0:T(8,128)} %pop.1, bf16[64,128,128]{2,1,0:T(8,128)(2,1)S(1)} %copy-done, s32[1,64]{1,0:T(1,128)S(1)} %bitcast.3, s32[1,64]{1,0:T(1,128)S(1)} %bitcast.4, f32[8,128,128]{2,1,0:T(8,128)S(1)} %copy-done.1, ...), custom_call_target="tpu_custom_call" | custom-call | tf_op jit(solution)/shard_map/wind_roof_step/pallas_call | solution.py:413
  28.9 0.6 %copy.10 = f32[8,3,128]{2,0,1:T(8,128)} copy(f32[8,3,128]{2,1,0:T(4,128)S(1)} %get-tuple-element.4) | data formatting | bytes 24576 | tf_op jit(solution)/shard_map/wind_roof_step/pallas_call | solution.py:413
  29.5 0.6 %copy.11 = f32[64,3,128]{2,0,1:T(8,128)} copy(f32[64,3,128]{2,1,0:T(4,128)S(1)} %get-tuple-element.5) | data formatting | bytes 196608 | tf_op jit(solution)/shard_map/wind_roof_step/pallas_call | solution.py:413
  30.2 1.4 %copy.13 = f32[19,8,32,128]{3,2,1,0:T(8,128)} copy(f32[19,8,32,128]{3,2,1,0:T(8,128)S(1)} %get-tuple-element.9) | data formatting | bytes 4980736
Async XLA Ops:
  0.6 1.6 %copy-start = (bf16[64,128,128]{2,1,0:T(8,128)(2,1)S(1)}, bf16[64,128,128]{2,1,0:T(8,128)(2,1)}, u32[]{:S(2)}) copy-start(bf16[64,128,128]{2,1,0:T(8,128)(2,1)} %rbf.1) | copy-start | bytes 6291460
  2.2 1.0 %copy-start.1 = (f32[8,128,128]{2,1,0:T(8,128)S(1)}, f32[8,128,128]{2,1,0:T(8,128)}, u32[]{:S(2)}) copy-start(f32[8,128,128]{2,1,0:T(8,128)} %comp.1) | copy-start | bytes 1572868
  3.3 0.8 %copy-start.2 = (f32[128,128]{1,0:T(8,128)S(1)}, f32[128,128]{1,0:T(8,128)}, u32[]{:S(2)}) copy-start(f32[128,128]{1,0:T(8,128)} %ncomp.1) | copy-start | bytes 196612
  4.1 0.7 %copy-start.3 = (s32[64,1]{0,1:T(1,128)S(1)}, s32[64,1]{0,1:T(1,128)}, u32[]{:S(2)}) copy-start(s32[64,1]{0,1:T(1,128)} %param.9) | copy-start | bytes 772
  4.8 0.7 %copy-start.4 = (s32[64,1]{0,1:T(1,128)S(1)}, s32[64,1]{0,1:T(1,128)}, u32[]{:S(2)}) copy-start(s32[64,1]{0,1:T(1,128)} %param.10) | copy-start | bytes 772
  5.4 0.7 %copy-start.5 = (s32[64]{0:T(128)S(1)}, s32[64]{0:T(128)}, u32[]{:S(2)}) copy-start(s32[64]{0:T(128)} %param.13) | copy-start | bytes 772

commit v2 on v1

--- a/solution.py
+++ b/solution.py
@@ -64,12 +64,12 @@
 
 def kernel(
     sizes,
-    pop, rbf, owner, slot, comp, ncomp, row,
-    out, disp, wall,
-    f, moments, grid, mom, weights, compliance, coupling,
+    pop, rbf, owner_in, slot_in, comp, ncomp, row_in,
+    grid, faces, disp, wall,
+    owner, slot, row, f, moments, mom, weights, compliance, coupling,
     gather, place, spread, traction, forces, part, recv, mine, shells,
-    xs, xr, ys, yr, zr,
-    in_sem, w_sem, ps_sem, pr_sem, ds_sem, dr_sem, hs_sem, hr_sem, zs_sem, zr_sem, o_sem,
+    xs, xr, ys, yr, zr, es, er,
+    in_sem, w_sem, ps_sem, pr_sem, ds_sem, dr_sem, hs_sem, hr_sem, zs_sem, zr_sem,
 ):
     gxn, gyn, gzn = sizes
     owners = gyn * gzn
@@ -94,6 +94,13 @@
     up = (gx, gy, step(gz, gzn, 1))
     down = (gx, gy, step(gz, gzn, -1))
 
+    small = [
+        pltpu.make_async_copy(row_in, row, w_sem.at[3]),
+        pltpu.make_async_copy(owner_in, owner, w_sem.at[4]),
+        pltpu.make_async_copy(slot_in, slot, w_sem.at[5]),
+    ]
+    for copy in small:
+        copy.start()
     loads_in = [pltpu.make_async_copy(pop.at[:, z], f.at[:, z], in_sem.at[z]) for z in range(depth)]
     for copy in loads_in:
         copy.start()
@@ -117,6 +124,9 @@
     for item in (left, right):
         pl.semaphore_signal(barrier, inc=1, device_id=item, device_id_type=MESH)
 
+    for copy in small:
+        copy.wait()
+
     square = iota((blocks, blocks), 0) == iota((blocks, blocks), 1)
 
     def down_rows(ref):
@@ -128,9 +138,9 @@
     ).astype(BF16)
     repeat = (iota((rows8, blocks), 0) // 8 == iota((rows8, blocks), 1)).astype(F32).astype(BF16)
     tall = dot(repeat, wide).astype(I32)
-    kind = iota((rows8, 128), 0) % 8
+    kind = iota((rows8, 1), 0) % 8
     row_key = tall[:, :128] + kind * cells
-    lane = iota((rows8, 128), 1)
+    lane = iota((1, 128), 1)
     for j in range(3 * cells // 128):
         hit = row_key == lane + 128 * j
         gather[:, j * 128 : (j + 1) * 128] = hit.astype(F32).astype(BF16)
@@ -148,7 +158,7 @@
     ).astype(I32)
     lane_kind = iota((1, rows8), 1) % 8
     lane_key = jnp.where(lane_kind < 3, lane_key + lane_kind, -100)
-    place_row = iota((owners * 32, rows8), 0)
+    place_row = iota((owners * 32, 1), 0)
     place_key = jnp.where(
         place_row % 32 < 3 * shell + 3,
         place_row // 32 * (3 * shell) - 3 + place_row % 32,
@@ -185,13 +195,19 @@
     traction[...] = dot(gather[...], mom[...])
     fixed[0].wait()
 
+    upper = iota((16, 128), 0) < 8
+
     def force(g, carry):
         for i in range(8):
-            at = pl.ds(pl.multiple_of(g * 64 + i * 8, 8), 8)
-            forces[at, :] = dot(traction[at, :].astype(BF16), weights[g * 8 + i])
-        return carry
-
-    lax.fori_loop(0, blocks // 8, force, 0)
+            at = pl.ds(pl.multiple_of(g * 128 + i * 16, 16), 16)
+            pair = traction[at, :]
+            pair = jnp.concatenate(
+                [jnp.where(upper, pair, 0.0), jnp.where(upper, 0.0, pair)], axis=1
+            ).astype(BF16)
+            forces[at, :] = dot(pair, weights[pl.ds(g * 16 + i * 2, 2)].reshape(256, 128))
+        return carry
+
+    lax.fori_loop(0, blocks // 16, force, 0)
     high, low = split(forces[...])
     both = dot(place[...], jnp.concatenate([high, low], axis=1))
     part[...] = (both[:, :128] + both[:, 128:]).reshape(owners, 32, 128)
@@ -288,7 +304,9 @@
         moved.append(a[:8] + a[8:] + b[:8])
     moved[1] = moved[1] + moved[0]
     for s in range(shell):
-        disp[s] = moved[s + 1][:3]
+        forces[s * 8 : s * 8 + 8, :] = moved[s + 1]
+    for k in range(3):
+        disp[k] = forces[pl.ds(k, shell, stride=8), :]
     r8, c8 = iota((32, 8 * shell), 0), iota((32, 8 * shell), 1)
     compact = ((c8 % 8 < 3) & (c8 // 8 * 3 + c8 % 8 == r8)).astype(F32).astype(BF16)
     rounded = jnp.concatenate(moved[1:], axis=0).astype(BF16)
@@ -319,25 +337,27 @@
     for d in range(5):
         ys[0, d] = grid[YP[d], :, height - 1, :]
         ys[1, d] = grid[YM[d], :, 0, :]
+    edges = []
+    for q in range(15, 19):
+        _, along_y, along_z = lattice_velocity[q]
+        side, d = (0, YP.index(q)) if along_y > 0 else (1, YM.index(q))
+        es[q - 15] = ys[side, d]
+        edges.append((q, along_y, along_z, (gx, step(gy, gyn, along_y), step(gz, gzn, along_z))))
     y_copies = [halo(ys.at[0], yr.at[0], 2, north), halo(ys.at[1], yr.at[1], 3, south)]
+    for q, along_y, along_z, device in edges:
+        line = depth - 1 if along_z > 0 else 0
+        es[q - 15, 0:1, :] = es[q - 15, line : line + 1, :]
+        y_copies.append(halo(es.at[q - 15], er.at[q - 15], q - 11, device))
     for copy in y_copies:
         copy.start()
-    ylane = iota((height, width), 0)
-
-    for copy in y_copies:
-        copy.wait_recv()
-
-    def shift_y(z, carry):
+
+    def roll_y(z, carry):
         for d in range(5):
-            q = YP[d]
-            grid[q, z] = jnp.where(ylane == 0, yr[0, d, pl.ds(z, 1), :], pltpu.roll(grid[q, z], 1, 0))
-            q = YM[d]
-            grid[q, z] = jnp.where(
-                ylane == height - 1, yr[1, d, pl.ds(z, 1), :], pltpu.roll(grid[q, z], height - 1, 0)
-            )
-        return carry
-
-    lax.fori_loop(0, depth, shift_y, 0)
+            grid[YP[d], z] = pltpu.roll(grid[YP[d], z], 1, 0)
+            grid[YM[d], z] = pltpu.roll(grid[YM[d], z], height - 1, 0)
+        return carry
+
+    lax.fori_loop(0, depth, roll_y, 0)
     z_copies = []
     for d in range(5):
         for side, q, z, device in ((0, ZP[d], depth - 1, up), (1, ZM[d], 0, down)):
@@ -349,17 +369,6 @@
                 )
             )
             z_copies[-1].start()
-    written = []
-
-    def write(src, dst):
-        written.append(pltpu.make_async_copy(src, dst, o_sem.at[len(written)]))
-        written[-1].start()
-
-    for q in NOT_Z:
-        write(grid.at[q], out.at[q])
-    for d in range(5):
-        write(grid.at[ZP[d], 0 : depth - 1], out.at[ZP[d], 1:depth])
-        write(grid.at[ZM[d], 1:depth], out.at[ZM[d], 0 : depth - 1])
 
     def take_disp(d, carry):
         other = lax.rem(me + d, owners)
@@ -372,21 +381,36 @@
 
     def motion(g, carry):
         for i in range(8):
-            at = pl.ds(pl.multiple_of(g * 64 + i * 8, 8), 8)
+            at = pl.ds(pl.multiple_of(g * 128 + i * 16, 16), 16)
             value = lax.dot_general(
-                traction[at, :].astype(BF16), weights[g * 8 + i],
+                traction[at, :].astype(BF16),
+                weights[pl.ds(g * 16 + i * 2, 2)].reshape(256, 128),
                 (((1,), (1,)), ((), ())), preferred_element_type=F32,
             )
-            wall[g * 8 + i] = value[:3]
-        return carry
-
-    lax.fori_loop(0, blocks // 8, motion, 0)
-
+            forces[at, :] = jnp.where(upper, value[:, :128], value[:, 128:])
+        return carry
+
+    lax.fori_loop(0, blocks // 16, motion, 0)
+    for k in range(3):
+        wall[k] = forces[pl.ds(k, blocks, stride=8), :]
+
+    for copy in y_copies:
+        copy.wait_recv()
+    for d in range(5):
+        for side, q, line in ((0, YP[d], 0), (1, YM[d], height - 1)):
+            along_z = lattice_velocity[q][2]
+            lo, hi = (1 if along_z < 0 else 0), (depth - 1 if along_z > 0 else depth)
+            for z in range(lo, hi):
+                grid[q, z, line : line + 1, :] = yr[side, d, z : z + 1, :]
     for copy in z_copies:
         copy.wait_recv()
     for d in range(5):
-        write(zr.at[0, d], out.at[ZP[d], 0])
-        write(zr.at[1, d], out.at[ZM[d], depth - 1])
+        faces[0, d] = zr[0, d]
+        faces[1, d] = zr[1, d]
+    for q, along_y, along_z, _ in edges:
+        side, d = (0, ZP.index(q)) if along_z > 0 else (1, ZM.index(q))
+        line = 0 if along_y > 0 else height - 1
+        faces[side, d, line : line + 1, :] = er[q - 15, 0:1, :]
 
     def drain(d, carry):
         other = lax.rem(me + d, owners)
@@ -397,7 +421,24 @@
     lax.fori_loop(1, owners, drain, 0)
     for copy in x_copies + y_copies + z_copies:
         copy.wait_send()
-    for copy in written:
+
+
+def assemble(grid, faces, disp, wall, out, disp_out, wall_out, sem):
+    depth = grid.shape[1]
+    moves = [(disp, disp_out), (wall, wall_out)]
+    for q in NOT_Z:
+        moves.append((grid.at[q], out.at[q]))
+    for d in range(5):
+        moves.append((grid.at[ZP[d], 0 : depth - 1], out.at[ZP[d], 1:depth]))
+        moves.append((grid.at[ZM[d], 1:depth], out.at[ZM[d], 0 : depth - 1]))
+        moves.append((faces.at[0, d], out.at[ZP[d], 0]))
+        moves.append((faces.at[1, d], out.at[ZM[d], depth - 1]))
+    copies = [
+        pltpu.make_async_copy(src, dst, sem.at[i]) for i, (src, dst) in enumerate(moves)
+    ]
+    for copy in copies:
+        copy.start()
+    for copy in copies:
         copy.wait()
 
 
@@ -407,22 +448,27 @@
     shell = comp.shape[0]
     owners = sizes[1] * sizes[2]
     rows8 = blocks * 8
-    any_space = pl.BlockSpec(memory_space=pl.ANY)
+    hbm = pl.BlockSpec(memory_space=pltpu.HBM)
     vmem = pl.BlockSpec(memory_space=pltpu.VMEM)
     dma = pltpu.SemaphoreType.DMA
-    return pl.pallas_call(
+    disp_shape = jax.ShapeDtypeStruct((3, shell, nodes), F32)
+    wall_shape = jax.ShapeDtypeStruct((3, blocks, width), F32)
+    parts = pl.pallas_call(
         functools.partial(kernel, sizes),
         out_shape=(
             jax.ShapeDtypeStruct(pop.shape, F32),
-            jax.ShapeDtypeStruct((shell, 3, nodes), F32),
-            jax.ShapeDtypeStruct((blocks, 3, width), F32),
+            jax.ShapeDtypeStruct((2, 5, height, width), F32),
+            disp_shape,
+            wall_shape,
         ),
-        in_specs=[any_space, any_space, vmem, vmem, any_space, any_space, vmem],
-        out_specs=(any_space, vmem, vmem),
+        in_specs=[hbm] * 7,
+        out_specs=(vmem,) * 4,
         scratch_shapes=[
+            pltpu.VMEM((1, blocks), I32),
+            pltpu.VMEM((1, blocks), I32),
+            pltpu.VMEM((1, blocks), I32),
             pltpu.VMEM(pop.shape, F32),
             pltpu.VMEM((4, depth, height, width), F32),
-            pltpu.VMEM(pop.shape, F32),
             pltpu.VMEM((3 * depth * height, width), BF16),
             pltpu.VMEM(rbf.shape, BF16),
             pltpu.VMEM(comp.shape, F32),
@@ -441,26 +487,42 @@
             pltpu.VMEM((2, 5, depth, width), F32),
             pltpu.VMEM((2, 5, depth, width), F32),
             pltpu.VMEM((2, 5, height, width), F32),
+            pltpu.VMEM((4, depth, width), F32),
+            pltpu.VMEM((4, depth, width), F32),
             dma((depth,)),
-            dma((3,)),
+            dma((6,)),
             dma((owners,)),
             dma((owners,)),
             dma((owners,)),
             dma((owners,)),
-            dma((4,)),
-            dma((4,)),
+            dma((8,)),
+            dma((8,)),
             dma((2, 5)),
             dma((2, 5)),
-            dma((len(NOT_Z) + 20,)),
         ],
         compiler_params=pltpu.CompilerParams(
             collective_id=0, has_side_effects=True, vmem_limit_bytes=48 * 1024 * 1024
         ),
         name="wind_roof_step",
     )(
-        pop, rbf, owner.reshape(1, blocks), slot.reshape(1, blocks), comp, ncomp,
-        row.reshape(1, blocks),
+        *(
+            pltpu.with_memory_space_constraint(item, pltpu.HBM)
+            for item in (
+                pop, rbf, owner.reshape(1, blocks), slot.reshape(1, blocks), comp, ncomp,
+                row.reshape(1, blocks),
+            )
+        )
     )
+    new, displacement, motion = pl.pallas_call(
+        assemble,
+        out_shape=(jax.ShapeDtypeStruct(pop.shape, F32), disp_shape, wall_shape),
+        in_specs=[vmem] * 4,
+        out_specs=(hbm,) * 3,
+        scratch_shapes=[dma((2 + len(NOT_Z) + 20,))],
+        compiler_params=pltpu.CompilerParams(vmem_limit_bytes=16 * 1024 * 1024),
+        name="assemble",
+    )(*parts)
+    return new, displacement.transpose(1, 0, 2), motion.transpose(1, 0, 2)
 
 
 def solution(mesh):

time: 31.9 us -> 21.4 us (0.67)
  the two profiles are of different devices: /device:TPU:1 before, /device:TPU:0 now
where the time goes in v2:
time: 21.4 us; the launch traced here: 21.3 us
  Pallas kernels  20.6 us (96%)
  between operations  0.64 us (3%)
    pallas_call x1, Pallas kernels, body(): pl.pallas_call(functools.partial(kernel, sizes), out_shape=(jax.ShapeDtyp...  18.9 us
    pallas_call x1, Pallas kernels, body(): pl.pallas_call(assemble, out_shape=(jax.ShapeDtypeStruct(pop.shape, F32),...  1.73 us

profile of v2, /device:TPU:0, one launch (start us, length us, event | category | flops | bytes accessed | tf_op | source)
XLA Modules:
  0.0 21.3 jit_solution(771083105109399589)
XLA Ops:
  0.6 18.9 %wind_roof_step.1 = (f32[19,8,32,128]{3,2,1,0:T(8,128)S(1)}, f32[2,5,32,128]{3,2,1,0:T(8,128)S(1)}, f32[3,8,128]{2,1,0:T(8,128)S(1)}, f32[3,64,128]{2,1,0:T(8,128)S(1)}) custom-call(f32[19,8,32,128]{3,2,1,0:T(8,128)} %pop.1, bf16[64,128,128]{2,1,0:T(8,128)(2,1)} %rbf.1, s32[1,64]{1,0:T(1,128)} %bitcast.5, s32[1,64]{1,0:T(1,128)} %bitcast.6, ...), custom_call_target="tpu_custom_call" | custom-call | tf_op jit(solution)/shard_map/wind_roof_step/pallas_call | solution.py:456
  19.6 1.7 %assemble.1 = (f32[19,8,32,128]{3,2,1,0:T(8,128)}, f32[3,8,128]{2,1,0:T(8,128)}, f32[3,64,128]{2,1,0:T(8,128)}) custom-call(f32[19,8,32,128]{3,2,1,0:T(8,128)S(1)} %get-tuple-element.10.grid, f32[2,5,32,128]{3,2,1,0:T(8,128)S(1)} %get-tuple-element.11.faces, f32[3,8,128]{2,1,0:T(8,128)S(1)} %get-tuple-element.12.disp, f32[3,64,128]{2,1,0:T(8,128)S(1)} %get-tuple-element.13.wall), custom_call_target="tpu_custom_call" | custom-call | tf_op jit(solution)/shard_map/assemble/pallas_call | solution.py:516
